TPU v7x, 512 devices: a whole 4x8x8 slice. The times are simulated.
512 devices in a mesh: prompt: 16 (over z_lo, x, core), resp: 32 (over y, z_hi).
Axes of the slice: x: 4, y: 8, z: 8 (z_hi: 4, z_lo: 2; z = z_hi * 2 + z_lo), core: 2. Of those that a mesh axis runs over, the one named last changes fastest.
Arguments:
- prefix_input: bfloat16 [16, 2048, 5120], P('prompt', 'resp'), may hold values from -6 to 6
- prefix_query_rows: bfloat16 [16, 2048, 2560], P('prompt', 'resp'), may hold values from -10 to 10
- prefix_key_rows: bfloat16 [16, 2048, 512], P('prompt', 'resp'), may hold values from -2.5 to 2.5
- prefix_value_rows: bfloat16 [16, 2048, 512], P('prompt', 'resp'), may hold values from -6 to 6
- prefix_output: bfloat16 [16, 2048, 2560], P('prompt', 'resp'), may hold values from -3 to 3
- prefix_output_grad: bfloat16 [16, 2048, 2560], P('prompt', 'resp'), may hold values from -6 to 6
- prefix_middle: bfloat16 [16, 2048, 64], P('prompt', 'resp'), may hold values from -6 to 6
- response_input: bfloat16 [16, 32, 64, 5120], P('prompt', 'resp'), may hold values from -6 to 6
- response_query: bfloat16 [16, 32, 64, 2560], P('prompt', 'resp'), may hold values from -10 to 10
- response_key: bfloat16 [16, 32, 64, 512], P('prompt', 'resp'), may hold values from -2.5 to 2.5
- response_value: bfloat16 [16, 32, 64, 512], P('prompt', 'resp'), may hold values from -6 to 6
- response_output: bfloat16 [16, 32, 64, 2560], P('prompt', 'resp'), may hold values from -3 to 3
- response_output_grad: bfloat16 [16, 32, 64, 2560], P('prompt', 'resp'), may hold values from -6 to 6
- response_middle: bfloat16 [16, 32, 64, 64], P('prompt', 'resp'), may hold values from -6 to 6
- lengths: int32 [16, 32], P('prompt', 'resp'), may hold values from 1 to 64, 1024 in all within a row
- adapter_up_weight: bfloat16 [64, 2560], replicated, may hold values from -0.75 to 0.75
Outputs:
- prefix_dkey: bfloat16 [16, 2048, 512], P('prompt', 'resp')
- prefix_dvalue: bfloat16 [16, 2048, 512], P('prompt', 'resp')
- resp_dkey: bfloat16 [16, 32, 64, 512], P('prompt', 'resp')
- resp_dvalue: bfloat16 [16, 32, 64, 512], P('prompt', 'resp')
- down_weight_grad: float32 [5120, 64], replicated
- up_weight_grad: float32 [64, 2560], replicated
Inputs may be any that keep to these rules, and one draw needn't show every extreme that they name: For each prompt the 32 lengths sum to 1024 and the longest is exactly 64.
All inputs are finite; a program needn't handle non-finite values. No bound on the sum of `lengths` on one device may be relied on, other than what follows from the above.
Results may differ from a plain program's by a relative error of at most 0.018.
Values may be sent and summed in bfloat16 or wider, within the bound.
A program may use at most 128 MiB of HBM per device.

v0:
```python
import jax
import jax.numpy as jnp
from jax import lax
from jax.sharding import PartitionSpec as P

HEAD_SIZE = 128


adapter_factor = 2.0


def local(
    prefix_input,
    prefix_query_rows,
    prefix_key_rows,
    prefix_value_rows,
    prefix_output,
    prefix_output_grad,
    prefix_middle,
    response_input,
    response_query,
    response_key,
    response_value,
    response_output,
    response_output_grad,
    response_middle,
    lengths,
    adapter_up_weight,
):
    kv_width = prefix_key_rows.shape[2]
    q_width = prefix_query_rows.shape[2]
    kv_heads = kv_width // HEAD_SIZE
    q_heads = q_width // HEAD_SIZE
    groups = q_width // kv_width
    rows_pre = prefix_query_rows.shape[1]
    rows_resp = response_query.shape[2]
    position = lax.axis_index("resp")
    keys_pre, values_pre = (
        lax.all_gather(prefix_key_rows[0], "resp", axis=0, tiled=True),
        lax.all_gather(prefix_value_rows[0], "resp", axis=0, tiled=True),
    )
    width_pre = keys_pre.shape[0]
    alive_rows = jnp.arange(rows_resp) < lengths[0, 0]
    own_grad = response_output_grad[0, 0]
    masked_grad = jnp.where(alive_rows[:, None], own_grad, jnp.zeros_like(own_grad))
    query_rows = jnp.concatenate([prefix_query_rows[0], response_query[0, 0]], axis=0)
    key_rows = jnp.concatenate([keys_pre, response_key[0, 0]], axis=0)
    value_rows = jnp.concatenate([values_pre, response_value[0, 0]], axis=0)
    grad_rows = jnp.concatenate([prefix_output_grad[0], masked_grad], axis=0)
    out_rows = jnp.concatenate([prefix_output[0], response_output[0, 0]], axis=0)
    total_rows = query_rows.shape[0]
    total_cols = key_rows.shape[0]
    row_index = jnp.arange(total_rows)[:, None]
    col_index = jnp.arange(total_cols)[None, :]
    prefix_col = col_index < width_pre
    pre_visible = prefix_col & (col_index <= position * rows_pre + row_index)
    resp_visible = prefix_col | (col_index - width_pre <= row_index - rows_pre)
    visible = jnp.where(row_index < rows_pre, pre_visible, resp_visible)
    scaling = HEAD_SIZE ** (-0.5)
    row_delta = jnp.sum(
        (grad_rows.astype(jnp.float32) * out_rows.astype(jnp.float32)).reshape(
            total_rows, q_heads, HEAD_SIZE
        ),
        axis=-1,
    )
    delta_heads = jnp.transpose(row_delta, (1, 0))
    query_heads = jnp.transpose(query_rows.reshape(total_rows, q_heads, HEAD_SIZE), (1, 0, 2))
    grad_heads = jnp.transpose(grad_rows.reshape(total_rows, q_heads, HEAD_SIZE), (1, 0, 2))
    key_heads = jnp.transpose(key_rows.reshape(total_cols, kv_heads, HEAD_SIZE), (1, 0, 2))
    value_heads = jnp.transpose(value_rows.reshape(total_cols, kv_heads, HEAD_SIZE), (1, 0, 2))
    group_index = jnp.arange(q_heads, dtype=jnp.int32) // groups
    contract_final_axis = (((1,), (1,)), ((), ()))

    def one_head(head_data):
        head_query, head_grad, head_delta, head_group = head_data
        head_key = lax.dynamic_index_in_dim(key_heads, head_group, 0, keepdims=False)
        head_value = lax.dynamic_index_in_dim(value_heads, head_group, 0, keepdims=False)
        scores = scaling * lax.dot_general(
            head_query, head_key, contract_final_axis, preferred_element_type=jnp.float32
        )
        scores = jnp.where(visible, scores, -jnp.inf)
        maxima = jnp.max(scores, axis=-1, keepdims=True)
        exp_terms = jnp.exp(scores - maxima)
        probs_full = exp_terms / jnp.sum(exp_terms, axis=-1, keepdims=True)
        probs_low = probs_full.astype(jnp.bfloat16)
        grad_probs = lax.dot_general(
            head_grad, head_value, contract_final_axis, preferred_element_type=jnp.float32
        )
        grad_scores = probs_full * (grad_probs - head_delta[:, None])
        scores_low = grad_scores.astype(jnp.bfloat16)
        head_dquery = scaling * jnp.dot(scores_low, head_key, preferred_element_type=jnp.float32)
        return (scores_low, probs_low, head_dquery)

    scores_all, probs_all, dquery_all = lax.map(
        one_head, (query_heads, grad_heads, delta_heads, group_index)
    )
    query_gradient = jnp.transpose(dquery_all, (1, 0, 2)).reshape(total_rows, q_width)
    scores_grouped = scores_all.reshape(kv_heads, groups, total_rows, total_cols)
    probs_grouped = probs_all.reshape(kv_heads, groups, total_rows, total_cols)
    query_grouped = query_heads.reshape(kv_heads, groups, total_rows, HEAD_SIZE)
    grad_grouped = grad_heads.reshape(kv_heads, groups, total_rows, HEAD_SIZE)

    def key_grads(start_col, col_count):
        scores_part = lax.dynamic_slice_in_dim(scores_grouped, start_col, col_count, 3)
        probs_part = lax.dynamic_slice_in_dim(probs_grouped, start_col, col_count, 3)
        grad_key = scaling * jnp.einsum(
            "kgrc,kgrd->ckd", scores_part, query_grouped, preferred_element_type=jnp.float32
        )
        grad_value = jnp.einsum(
            "kgrc,kgrd->ckd", probs_part, grad_grouped, preferred_element_type=jnp.float32
        )
        return (grad_key.reshape(col_count, kv_width), grad_value.reshape(col_count, kv_width))

    key_terms, value_terms = key_grads(0, width_pre)
    own_key, own_value = (
        lax.psum_scatter(
            key_terms.astype(jnp.bfloat16), "resp", scatter_dimension=0, tiled=True
        ).astype(jnp.float32),
        lax.psum_scatter(
            value_terms.astype(jnp.bfloat16), "resp", scatter_dimension=0, tiled=True
        ).astype(jnp.float32),
    )
    resp_key_grad, resp_value_grad = key_grads(width_pre, rows_resp)
    query_reduced = query_gradient.astype(jnp.bfloat16)
    middle_rows = jnp.concatenate([prefix_middle[0], response_middle[0, 0]], axis=0)
    input_arrays = jnp.concatenate([prefix_input[0], response_input[0, 0]], axis=0)
    up_piece = lax.dot_general(
        middle_rows, query_reduced, (((0,), (0,)), ((), ())), preferred_element_type=jnp.float32
    )
    hidden_reduced = lax.dot_general(
        query_reduced, adapter_up_weight, contract_final_axis, preferred_element_type=jnp.float32
    ).astype(jnp.bfloat16)
    down_piece = lax.dot_general(
        input_arrays, hidden_reduced, (((0,), (0,)), ((), ())), preferred_element_type=jnp.float32
    )
    down_grad_total, up_grad_total = lax.psum((down_piece, up_piece), ("prompt", "resp"))
    return (
        own_key.astype(jnp.bfloat16)[None],
        own_value.astype(jnp.bfloat16)[None],
        resp_key_grad.astype(jnp.bfloat16)[None, None],
        resp_value_grad.astype(jnp.bfloat16)[None, None],
        adapter_factor * down_grad_total,
        adapter_factor * up_grad_total,
    )


def solution(mesh):
    return jax.shard_map(
        local,
        mesh=mesh,
        in_specs=(
            P("prompt", "resp", None),
            P("prompt", "resp", None),
            P("prompt", "resp", None),
            P("prompt", "resp", None),
            P("prompt", "resp", None),
            P("prompt", "resp", None),
            P("prompt", "resp", None),
            P("prompt", "resp", None, None),
            P("prompt", "resp", None, None),
            P("prompt", "resp", None, None),
            P("prompt", "resp", None, None),
            P("prompt", "resp", None, None),
            P("prompt", "resp", None, None),
            P("prompt", "resp", None, None),
            P("prompt", "resp"),
            P(),
        ),
        out_specs=(
            P("prompt", "resp", None),
            P("prompt", "resp", None),
            P("prompt", "resp", None, None),
            P("prompt", "resp", None, None),
            P(),
            P(),
        ),
        check_vma=False,
    )
```

profile of v0, /device:TPU:2, one launch (start us, length us, event | category | flops | bytes accessed | tf_op | source)
XLA Modules:
  0.0 1123.4 jit_solution(1985111534883341308)
XLA Ops:
  21.7 81.7 %all-gather.5.cloned.1.call-done = bf16[1,2048,512]{2,1,0:T(8,128)(2,1)} async-done(((bf16[1,64,512]{2,1,0:T(8,128)(2,1)}), bf16[1,2048,512]{2,1,0:T(8,128)(2,1)}) %all-gather.5.cloned.1.call-update) | async-done | bytes 2097168 | tf_op jit(solution)/shard_map/all_gather | solution.py:39
  103.4 2.9 copy.54
  107.9 3.1 copy.59
  111.0 78.5 %all-gather.7.cloned.1.call-done = bf16[1,2048,512]{2,1,0:T(8,128)(2,1)} async-done(((bf16[1,64,512]{2,1,0:T(8,128)(2,1)}), bf16[1,2048,512]{2,1,0:T(8,128)(2,1)}) %all-gather.7.cloned.1.call-update) | async-done | bytes 2097168 | tf_op jit(solution)/shard_map/all_gather | solution.py:40
  189.6 4.0 copy.56
  193.5 3.2 maximum_bitcast_fusion.1
  196.7 4.1 copy.61
  200.9 172.5 %while.15 = (s32[]{:T(128)}, bf16[20,128,2112]{1,2,0:T(8,128)(2,1)}, bf16[20,128,2112]{1,2,0:T(8,128)(2,1)}, bf16[20,128,128]{1,2,0:T(8,128)(2,1)}, bf16[20,128,...) while((s32[]{:T(128)}, ...), condition=%wide.region_4.5_spmd.clone, body=%wide.region_1.4_spmd.clone.sunk | while | flops 212516608 | bytes 8363251 | solution.py:94
  206.2 2.2 bitcast_dynamic-update-slice_fusion.4
  214.8 2.2 bitcast_dynamic-update-slice_fusion.4
  223.4 2.3 bitcast_dynamic-update-slice_fusion.4
  232.0 2.3 bitcast_dynamic-update-slice_fusion.4
  258.0 2.3 bitcast_dynamic-update-slice_fusion.4
  266.7 2.3 bitcast_dynamic-update-slice_fusion.4
  275.3 2.2 bitcast_dynamic-update-slice_fusion.4
  283.9 2.2 bitcast_dynamic-update-slice_fusion.4
  309.7 2.3 bitcast_dynamic-update-slice_fusion.4
  335.6 2.2 bitcast_dynamic-update-slice_fusion.4
  344.2 2.3 bitcast_dynamic-update-slice_fusion.4
  361.5 2.2 bitcast_dynamic-update-slice_fusion.4
  370.1 2.3 bitcast_dynamic-update-slice_fusion.4
  373.5 2.3 fusion.45
  375.8 3.2 fusion.33
  379.5 14.5 %copy.63 = bf16[20,128,2112]{2,1,0:T(8,128)(2,1)} copy(bf16[20,128,2112]{1,2,0:T(8,128)(2,1)} %get-tuple-element.65) | data formatting | bytes 21626880 | tf_op jit(solution)/shard_map/while | solution.py:94
  394.0 7.3 fusion.28
  401.2 3.9 copy.64
  405.9 14.5 %copy.66 = bf16[20,128,2112]{2,1,0:T(8,128)(2,1)} copy(bf16[20,128,2112]{1,2,0:T(8,128)(2,1)} %get-tuple-element.66) | data formatting | bytes 21626880 | tf_op jit(solution)/shard_map/while | solution.py:94
  420.4 7.3 bitcast_convert_fusion
  427.7 3.9 copy.67
  436.2 216.6 %all-reduce.3.cloned.1.call-done = (f32[5120,64]{0,1:T(8,128)}, f32[64,2560]{1,0:T(8,128)}) async-done(((f32[5120,64]{0,1:T(8,128)}, f32[64,2560]{1,0:T(8,128)}), (f32[5120,64]{0,1:T(8,128)}, f32[64,2560]{1,0:T(8,128)})) %all-reduce.3.cloned.1.call-update) | async-done | bytes 1966096 | tf_op jit(solution)/shard_map/psum | solution.py:136
  656.0 229.5 %reduce-scatter.3.cloned.1.call-done = bf16[64,512]{1,0:T(8,128)(2,1)} async-done(((bf16[2048,512]{1,0:T(8,128)(2,1)}), bf16[64,512]{1,0:T(8,128)(2,1)}) %reduce-scatter.3.cloned.1.call-update) | async-done | bytes 65552 | tf_op jit(solution)/shard_map/reduce_scatter | solution.py:116
  885.5 231.3 %reduce-scatter.5.cloned.1.call-done = bf16[64,512]{1,0:T(8,128)(2,1)} async-done(((bf16[2048,512]{1,0:T(8,128)(2,1)}), bf16[64,512]{1,0:T(8,128)(2,1)}) %reduce-scatter.5.cloned.1.call-update) | async-done | bytes 65552 | tf_op jit(solution)/shard_map/reduce_scatter | solution.py:119
  (242 shorter events, 128.2 us)
Async XLA Ops:
  7.2 368.6 %copy-start = (bf16[64,2560]{1,0:T(8,128)(2,1)S(1)}, bf16[64,2560]{1,0:T(8,128)(2,1)}, u32[]{:S(2)}) copy-start(bf16[64,2560]{1,0:T(8,128)(2,1)} %param.33) | copy-start | bytes 983044
  7.2 6.5 copy-start.5
  7.2 6.8 copy-start.6
  7.2 7.0 copy-start.7
  7.2 96.2 %all-gather.5.cloned.1.call-start = ((), (), s32[]{:S(2)}) async-start(), calls=%async_computation.4 | async-start | bytes 2162688 | tf_op jit(solution)/shard_map/all_gather | solution.py:39
  7.9 181.6 %all-gather.7.cloned.1.call-start = ((), (), s32[]{:S(2)}) async-start(), calls=%async_computation.5 | async-start | bytes 2162688 | tf_op jit(solution)/shard_map/all_gather | solution.py:40
  8.7 644.1 %all-reduce.3.cloned.1.call-start = ((), (), s32[]{:S(2)}) async-start(), calls=%async_computation.6 | async-start | bytes 3932160 | tf_op jit(solution)/shard_map/psum | solution.py:136
  17.5 0.9 copy-start.2
  196.7 4.2 copy-start.10
  196.7 4.2 copy-start.11
  196.7 4.2 copy-start.12
  196.7 4.2 copy-start.13
  196.7 4.2 copy-start.14
  200.9 172.6 %copy-start.8 = (bf16[1,1,64,64]{3,2,1,0:T(8,128)(2,1)S(1)}, bf16[1,1,64,64]{3,2,1,0:T(8,128)(2,1)}, u32[]{:S(2)}) copy-start(bf16[1,1,64,64]{3,2,1,0:T(8,128)(2,1)} %param.31) | copy-start | bytes 24580
  200.9 172.6 %copy-start.9 = (bf16[1,64,64]{2,1,0:T(8,128)(2,1)S(1)}, bf16[1,64,64]{2,1,0:T(8,128)(2,1)}, u32[]{:S(2)}) copy-start(bf16[1,64,64]{2,1,0:T(8,128)(2,1)} %param.24) | copy-start | bytes 24580
  375.8 3.2 copy-start.3
  379.0 506.6 %reduce-scatter.3.cloned.1.call-start = ((), (), s32[]{:S(2)}) async-start(), calls=%async_computation.2 | async-start | bytes 2162688 | tf_op jit(solution)/shard_map/reduce_scatter | solution.py:116
  405.2 711.6 %reduce-scatter.5.cloned.1.call-start = ((), (), s32[]{:S(2)}) async-start(), calls=%async_computation.3 | async-start | bytes 2162688 | tf_op jit(solution)/shard_map/reduce_scatter | solution.py:119
  433.9 683.0 %copy-start.1 = (bf16[64,2560]{1,0:T(8,128)(2,1)S(1)}, bf16[64,2560]{1,0:T(8,128)(2,1)}, u32[]{:S(2)}) copy-start(bf16[64,2560]{1,0:T(8,128)(2,1)} %param.33) | copy-start | bytes 983044
  652.8 2.1 copy-start.4
Sparse Core Ops, SparseCore 0:
  11.2 92.1 all-gather.4
  106.6 82.9 all-gather.6
  379.1 273.6 all-reduce.2
  658.4 227.1 reduce-scatter.2
  890.4 226.3 reduce-scatter.4
where the time goes:
time: 1130 us; the launch traced here: 1120 us
  waiting for transfers between devices  839 us (74%)
  matrix products  103 us (9%)
  local copies, waits for them, and re-layouts  89.2 us (8%)
  loops' own time  39.4 us (3%)
  other arithmetic  37.2 us (3%)
  between operations  14.7 us (1%)
    reduce_scatter x1, waiting for transfers between devices, local(): lax.psum_scatter(value_terms.astype(jnp.bfloat16), 'resp', scatter_dimens...  231 us
    reduce_scatter x1, waiting for transfers between devices, local(): lax.psum_scatter(key_terms.astype(jnp.bfloat16), 'resp', scatter_dimensio...  229 us
    psum x1, waiting for transfers between devices, local(): lax.psum((down_piece, up_piece), ('prompt', 'resp'))  217 us
    all_gather x1, waiting for transfers between devices, local(): lax.all_gather(prefix_key_rows[0], 'resp', axis=0, tiled=True)  81.7 us
    all_gather x1, waiting for transfers between devices, local(): lax.all_gather(prefix_value_rows[0], 'resp', axis=0, tiled=True)  78.5 us
    dot_general x20, matrix products, one_head(): lax.dot_general(head_grad, head_value, contract_final_axis, preferred_ele...  45 us
    another operation x1, loops' own time, local(): lax.map(one_head, (query_heads, grad_heads, delta_heads, group_index))  39.4 us
    while x2, local copies, waits for them, and re-layouts, local(): lax.map(one_head, (query_heads, grad_heads, delta_heads, group_index))  29 us
  transfers between devices with their start and end apart: 5, of which 5 were waited for; matrix products, arithmetic and copies ran while one was open for 7% of the time, Pallas kernels for 0%

commit v1 on v0

v1 whole, which is shorter than its diff:
```python
import functools
import math

import jax
import jax.numpy as jnp
from jax import lax
from jax.experimental import pallas as pl
from jax.experimental.pallas import tpu as pltpu
from jax.sharding import PartitionSpec as P

ZL, X, C, Y, ZH = 2, 4, 2, 8, 4
HD = 128
ROWS = 64
KVH = 4
GROUPS = 5
RANK = 64
LANES = 512
GROUP_LANES = GROUPS * HD
QL = 2 * ROWS * GROUPS
SCALE = HD ** -0.5
LOG2E = math.log2(math.e)
F32 = jnp.float32
BF16 = jnp.bfloat16
MESH = pl.DeviceIdType.MESH


def mod(a, n):
    return lax.rem(a + n, n)


def nt(a, b):
    return lax.dot_general(a, b, (((1,), (1,)), ((), ())), preferred_element_type=F32)


def nn(a, b):
    return lax.dot_general(a, b, (((1,), (0,)), ((), ())), preferred_element_type=F32)


def tn(a, b):
    return lax.dot_general(a, b, (((0,), (0,)), ((), ())), preferred_element_type=F32)


class Place:
    def __init__(self):
        p, r = lax.axis_index("prompt"), lax.axis_index("resp")
        self.p, self.r = p, r
        self.core = lax.rem(p, C)
        self.x = lax.rem(lax.div(p, C), X)
        self.zl = lax.div(p, C * X)
        self.y = lax.div(r, ZH)
        self.zh = lax.rem(r, ZH)
        self.z = self.zh * ZL + self.zl

    def device(self, core=None, x=None, y=None, z=None):
        core = self.core if core is None else core
        x = self.x if x is None else x
        y = self.y if y is None else y
        z = self.z if z is None else z
        zl, zh = lax.rem(z, ZL), lax.div(z, ZL)
        return {"prompt": (zl * X + x) * C + core, "resp": y * ZH + zh}


def entry_barrier(at):
    barrier = pltpu.get_barrier_semaphore()
    count = 0
    for off in range(1, C):
        pl.semaphore_signal(barrier, inc=1, device_id=at.device(core=mod(at.core + off, C)), device_id_type=MESH)
        count += 1
    for off in range(1, X):
        pl.semaphore_signal(barrier, inc=1, device_id=at.device(x=mod(at.x + off, X)), device_id_type=MESH)
        count += 1
    for off in range(1, Y):
        pl.semaphore_signal(barrier, inc=1, device_id=at.device(y=mod(at.y + off, Y)), device_id_type=MESH)
        count += 1
    for off in range(1, ZH * ZL):
        pl.semaphore_signal(barrier, inc=1, device_id=at.device(z=mod(at.z + off, ZH * ZL)), device_id_type=MESH)
        count += 1
    pl.semaphore_wait(barrier, count)


def rcopy(src, dst, send, recv, device):
    return pltpu.make_async_remote_copy(
        src_ref=src, dst_ref=dst, send_sem=send, recv_sem=recv, device_id=device, device_id_type=MESH)


def rows_at(start, count):
    return pl.ds(pl.multiple_of(start, ROWS), count)


def each(n, body):
    def step(i, carry):
        body(i)
        return carry
    lax.fori_loop(0, n, step, 0)


class Gather:
    def __init__(self, at, kv, zs, zr, ys, yr):
        self.at, self.kv, self.zs, self.zr, self.ys, self.yr = at, kv, zs, zr, ys, yr
        self.block = ZH * ROWS

    def z_copy(self, g, off, sending):
        at = self.at
        zh = at.zh if sending else mod(at.zh - off, ZH)
        ref = self.kv.at[g, :, rows_at((at.y * ZH + zh) * ROWS, ROWS), :]
        target = at.device(z=mod(at.zh + off, ZH) * ZL + at.zl)
        return rcopy(ref, ref, self.zs.at[g, off - 1], self.zr.at[g, off - 1], target)

    def y_copy(self, g, s, which, sending):
        at = self.at
        lag = s if sending else s + 1
        blk = mod(at.y - lag, Y) if which == 0 else mod(at.y + lag, Y)
        to = mod(at.y + 1, Y) if which == 0 else mod(at.y - 1, Y)
        ref = self.kv.at[g, which, rows_at(blk * self.block, self.block), :]
        return rcopy(ref, ref, self.ys.at[g, s, which], self.yr.at[g, s, which], at.device(y=to))

    def z_start(self, g):
        for off in range(1, ZH):
            self.z_copy(g, off, True).start()

    def z_wait(self, g):
        for off in range(1, ZH):
            self.z_copy(g, off, False).wait_recv()

    def y_start(self, g, s):
        for which in range(2):
            self.y_copy(g, s, which, True).start()

    def y_wait(self, g, s):
        for which in range(2):
            self.y_copy(g, s, which, False).wait_recv()

    def wait_sends(self, g):
        for off in range(1, ZH):
            self.z_copy(g, off, True).wait_send()
        for s in range(Y - 1):
            for which in range(2):
                self.y_copy(g, s, which, True).wait_send()


class Scatter:
    def __init__(self, at, tm, rb, zb, ss, sr, ws, wr):
        self.at, self.tm, self.rb, self.zb = at, tm, rb, zb
        self.ss, self.sr, self.ws, self.wr = ss, sr, ws, wr
        self.block = ZH * ROWS

    def rows(self, s, which):
        at = self.at
        blk = mod(at.y - 1 - s + Y, Y) if which == 0 else mod(at.y + 1 + s, Y)
        return rows_at(blk * self.block, self.block)

    def y_copy(self, g, s, which):
        at = self.at
        to = mod(at.y + 1, Y) if which == 0 else mod(at.y - 1, Y)
        return rcopy(self.tm.at[g, which, self.rows(s, which), :], self.rb.at[g, s, which],
                     self.ss.at[g, s, which], self.sr.at[g, s, which], at.device(y=to))

    def y_step(self, g, s):
        for which in range(2):
            if s > 0:
                self.y_copy(g, s - 1, which).wait_recv()
                rows = self.rows(s, which)
                total = self.tm[g, which, rows, :].astype(F32) + self.rb[g, s - 1, which].astype(F32)
                self.tm[g, which, rows, :] = total.astype(BF16)
            if s < Y - 1:
                self.y_copy(g, s, which).start()

    def z_copy(self, g, off):
        at = self.at
        zh = mod(at.zh + off, ZH)
        src = self.tm.at[g, :, rows_at((at.y * ZH + zh) * ROWS, ROWS), :]
        return rcopy(src, self.zb.at[g, off - 1], self.ws.at[g, off - 1], self.wr.at[g, off - 1],
                     at.device(z=zh * ZL + at.zl))

    def z_start(self, g):
        for off in range(1, ZH):
            self.z_copy(g, off).start()

    def finish(self, g, outs):
        at = self.at
        for off in range(1, ZH):
            self.z_copy(g, off).wait_recv()
        for which in range(2):
            total = self.tm[g, which, rows_at(at.r * ROWS, ROWS), :].astype(F32)
            for off in range(1, ZH):
                total += self.zb[g, off - 1, which].astype(F32)
            outs[which][:, pl.ds(pl.multiple_of(g * HD, HD), HD)] = total.astype(BF16)

    def wait_sends(self, g):
        for off in range(1, ZH):
            self.z_copy(g, off).wait_send()
        for s in range(Y - 1):
            for which in range(2):
                self.y_copy(g, s, which).wait_send()


class Reduce:
    def __init__(self, at, src, out, rc, rx, ry, rz, part, send, recv):
        self.at, self.src, self.out = at, src, out
        self.rc, self.rx, self.ry, self.rz, self.part = rc, rx, ry, rz, part
        self.send, self.recv = send, recv
        self.half = Y * LANES
        self.pending = []

    def rows(self, x):
        return pl.ds(pl.multiple_of(x * 16, 16), 16)

    def lanes(self, core, y=None):
        if y is None:
            return pl.ds(pl.multiple_of(core * self.half, LANES), self.half)
        return pl.ds(pl.multiple_of(core * self.half + y * LANES, LANES), LANES)

    def core_copy(self):
        at = self.at
        other = mod(at.core + 1, C)
        return rcopy(self.src.at[:, self.lanes(other)], self.rc, self.send.at[0, 0], self.recv.at[0, 0],
                     at.device(core=other))

    def x_copy(self, off):
        x = mod(self.at.x + off, X)
        return rcopy(self.part.at[self.rows(x), :], self.rx.at[off - 1], self.send.at[1, off - 1],
                     self.recv.at[1, off - 1], self.at.device(x=x))

    def y_copy(self, off):
        y = mod(self.at.y + off, Y)
        return rcopy(self.part.at[self.rows(self.at.x), pl.ds(pl.multiple_of(y * LANES, LANES), LANES)],
                     self.ry.at[off - 1], self.send.at[2, off - 1], self.recv.at[2, off - 1], self.at.device(y=y))

    def z_copy(self, off, sending):
        n = ZH * ZL
        z = self.at.z if sending else mod(self.at.z - off, n)
        return rcopy(self.rz.at[z], self.rz.at[z], self.send.at[3, off - 1], self.recv.at[3, off - 1],
                     self.at.device(z=mod(self.at.z + off, n)))

    def y_back(self, off, sending):
        y = self.at.y if sending else mod(self.at.y - off, Y)
        ref = self.out.at[self.rows(self.at.x), self.lanes(self.at.core, y)]
        return rcopy(ref, ref, self.send.at[4, off - 1], self.recv.at[4, off - 1],
                     self.at.device(y=mod(self.at.y + off, Y)))

    def x_back(self, off, sending):
        x = self.at.x if sending else mod(self.at.x - off, X)
        ref = self.out.at[self.rows(x), self.lanes(self.at.core)]
        return rcopy(ref, ref, self.send.at[5, off - 1], self.recv.at[5, off - 1],
                     self.at.device(x=mod(self.at.x + off, X)))

    def core_back(self, sending):
        core = self.at.core if sending else mod(self.at.core + 1, C)
        ref = self.out.at[:, self.lanes(core)]
        return rcopy(ref, ref, self.send.at[6, 0], self.recv.at[6, 0], self.at.device(core=mod(self.at.core + 1, C)))

    def steps(self):
        at = self.at
        n = ZH * ZL
        mine = lambda: (self.rows(at.x), pl.ds(pl.multiple_of(at.y * LANES, LANES), LANES))

        def core_start():
            self.core_copy().start()

        def x_start():
            self.core_copy().wait_recv()
            self.part[...] = (self.src[:, self.lanes(at.core)].astype(F32) + self.rc[...].astype(F32)).astype(BF16)
            for off in range(1, X):
                self.x_copy(off).start()

        def y_start():
            total = self.part[self.rows(at.x), :].astype(F32)
            for off in range(1, X):
                self.x_copy(off).wait_recv()
                total += self.rx[off - 1].astype(F32)
            self.part[self.rows(at.x), :] = total.astype(BF16)
            for off in range(1, Y):
                self.y_copy(off).start()

        def z_start():
            rows, lanes = mine()
            total = self.part[rows, lanes].astype(F32)
            for off in range(1, Y):
                self.y_copy(off).wait_recv()
                total += self.ry[off - 1].astype(F32)
            self.rz[at.z] = total.astype(BF16)
            for off in range(1, n):
                self.z_copy(off, True).start()

        def back_y():
            for off in range(1, n):
                self.z_copy(off, False).wait_recv()
            total = self.rz[0].astype(F32)
            for z in range(1, n):
                total += self.rz[z].astype(F32)
            self.out[self.rows(at.x), self.lanes(at.core, at.y)] = total.astype(BF16)
            for off in range(1, Y):
                self.y_back(off, True).start()

        def back_x():
            for off in range(1, Y):
                self.y_back(off, False).wait_recv()
            for off in range(1, X):
                self.x_back(off, True).start()

        def back_core():
            for off in range(1, X):
                self.x_back(off, False).wait_recv()
            self.core_back(True).start()

        def end():
            self.core_back(False).wait_recv()
            self.core_copy().wait_send()
            self.core_back(True).wait_send()
            for off in range(1, X):
                self.x_copy(off).wait_send()
                self.x_back(off, True).wait_send()
            for off in range(1, Y):
                self.y_copy(off).wait_send()
                self.y_back(off, True).wait_send()
            for off in range(1, n):
                self.z_copy(off, True).wait_send()

        return [core_start, x_start, y_start, z_start, back_y, back_x, back_core, end]


def attention(g, at, length, refs, kv, tm, scr):
    (pq, rq, pdo, rdo, po, ro, rk, rv) = refs
    (qs, dos, s_scr, e_scr, t_scr, dq_scr, rdk, rdv, hid, up_w, mid_t, ar_src) = scr
    chunk = ZH * ROWS
    prefix = Y * chunk
    base = pl.multiple_of(g * GROUP_LANES, HD)
    head_lanes = pl.ds(pl.multiple_of(g * HD, HD), HD)
    alive = lax.broadcasted_iota(jnp.int32, (ROWS, HD), 0) < length

    deltas = []
    for h in range(GROUPS):
        lanes = pl.ds(pl.multiple_of(base + h * HD, HD), HD)
        top, low = pl.ds(2 * h * ROWS, ROWS), pl.ds((2 * h + 1) * ROWS, ROWS)
        qs[top, :] = pq[:, lanes]
        qs[low, :] = rq[:, lanes]
        grad_top = pdo[:, lanes].astype(F32)
        grad_low = jnp.where(alive, rdo[:, lanes].astype(F32), 0.0)
        dos[top, :] = grad_top.astype(BF16)
        dos[low, :] = grad_low.astype(BF16)
        both = jnp.concatenate([grad_top * po[:, lanes].astype(F32), grad_low * ro[:, lanes].astype(F32)], axis=0)
        deltas.append(jnp.sum(both.T, axis=0, keepdims=True))
    delta = jnp.concatenate(deltas, axis=1)
    q, do = qs[...], dos[...]

    lane = lax.broadcasted_iota(jnp.int32, (1, QL), 1)
    in_head = lax.rem(lane, 2 * ROWS)
    limit = jnp.where(in_head < ROWS, at.r * ROWS + in_head, prefix)
    own_limit = in_head - ROWS
    row = lax.broadcasted_iota(jnp.int32, (chunk, QL), 0)
    own_row = lax.broadcasted_iota(jnp.int32, (ROWS, QL), 0)

    def top8(s, op):
        return op(s.reshape(s.shape[0] // 8, 8, QL), axis=0)

    s = jnp.where(own_row <= own_limit, nt(rk[:, head_lanes], q), -jnp.inf)
    s_scr[pl.ds(prefix, ROWS), :] = s

    def scores(c, m8):
        at_c = rows_at(c * chunk, chunk)
        s = jnp.where(row + c * chunk <= limit, nt(kv[g, 0, at_c, :], q), -jnp.inf)
        s_scr[at_c, :] = s
        return jnp.maximum(m8, top8(s, jnp.max))

    m8 = lax.fori_loop(0, Y, scores, top8(s, jnp.max))
    m = jnp.max(m8, axis=0, keepdims=True) * (SCALE * LOG2E)

    def weights(at_c, k, v):
        e = jnp.exp2(s_scr[at_c, :] * (SCALE * LOG2E) - m)
        t = (e * (nt(v, do) - delta)).astype(BF16)
        e_scr[at_c, :] = e.astype(BF16)
        t_scr[at_c, :] = t
        return top8(e, jnp.sum), tn(k, t)

    def back(c, carry):
        at_c = rows_at(c * chunk, chunk)
        l8, dq = weights(at_c, kv[g, 0, at_c, :], kv[g, 1, at_c, :])
        return carry[0] + l8, carry[1] + dq

    l8, dq = lax.fori_loop(0, Y, back, weights(pl.ds(prefix, ROWS), rk[:, head_lanes], rv[:, head_lanes]))
    inv = 1.0 / jnp.sum(l8, axis=0, keepdims=True)
    inv_col = jnp.concatenate(
        [jnp.broadcast_to(inv[:, h * HD:(h + 1) * HD], (HD, HD)).T for h in range(GROUPS)], axis=0)
    q_n = (q.astype(F32) * (inv_col * SCALE)).astype(BF16)
    do_n = (do.astype(F32) * inv_col).astype(BF16)
    dq_low = (dq * (inv * SCALE)).astype(BF16)

    def terms(c, carry):
        at_c = rows_at(c * chunk, chunk)
        tm[g, 0, at_c, :] = nn(t_scr[at_c, :], q_n).astype(BF16)
        tm[g, 1, at_c, :] = nn(e_scr[at_c, :], do_n).astype(BF16)
        return carry

    lax.fori_loop(0, Y, terms, 0)
    own = pl.ds(prefix, ROWS)
    rdk[:, head_lanes] = nn(t_scr[own, :], q_n).astype(BF16)
    rdv[:, head_lanes] = nn(e_scr[own, :], do_n).astype(BF16)

    hidden = hid[...]
    for h in range(GROUPS):
        lanes = pl.ds(pl.multiple_of(base + h * HD, HD), HD)
        part = dq_low[:, h * HD:(h + 1) * HD]
        hidden += nn(up_w[:, lanes], part)
        ar_src[:, pl.ds(pl.multiple_of(10 * LANES + base + h * HD, HD), HD)] = nt(mid_t, part).astype(BF16)
    hid[...] = hidden


def down_terms(hid, px, rx, ar_src):
    hidden = hid[...].astype(BF16)
    width = px.shape[1]
    for j in range(0, width, LANES):
        lanes = slice(j, j + LANES)
        ar_src[:, lanes] = (nn(hidden[:, :ROWS], px[:, lanes]) + nn(hidden[:, ROWS:], rx[:, lanes])).astype(BF16)
    ar_src[:, 15 * LANES:] = jnp.zeros((RANK, LANES), BF16)


def kernel(length_ref, pk, pv, rk, rv, pq, rq, pdo, rdo, po, ro, px, rx, pm, rm, up_w,
           pdk, pdv, rdk, rdv, total,
           kv, tm, rb, zb, qs, dos, s_scr, e_scr, t_scr, dq_scr, hid, ar_src, rc, rx_b, ry, rz, part,
           zs, zr, ys, yr, ss, sr, ws, wr, asend, arecv):
    at = Place()
    gather = Gather(at, kv, zs, zr, ys, yr)
    scatter = Scatter(at, tm, rb, zb, ss, sr, ws, wr)
    reduce = Reduce(at, ar_src, total, rc, rx_b, ry, rz, part, asend, arecv)

    for g in range(KVH):
        kv[g, 0, rows_at(at.r * ROWS, ROWS), :] = pk[:, g * HD:(g + 1) * HD]
        kv[g, 1, rows_at(at.r * ROWS, ROWS), :] = pv[:, g * HD:(g + 1) * HD]
    entry_barrier(at)
    each(KVH, gather.z_start)

    def first(g):
        gather.z_wait(g)
        gather.y_start(g, 0)
    each(KVH, first)
    for s in range(1, Y - 1):
        def pass_on(g, s=s):
            gather.y_wait(g, s - 1)
            gather.y_start(g, s)
        each(KVH, pass_on)
    each(KVH, lambda g: gather.y_wait(g, Y - 2))

    hid[...] = jnp.zeros_like(hid)
    mid_t = jnp.concatenate([pm[...].astype(F32).T, rm[...].astype(F32).T], axis=1).astype(BF16)
    refs = (pq, rq, pdo, rdo, po, ro, rk, rv)
    scr = (qs, dos, s_scr, e_scr, t_scr, dq_scr, rdk, rdv, hid, up_w, mid_t, ar_src)
    each(KVH, lambda g: attention(g, at, length_ref[0, 0], refs, kv, tm, scr))
    down_terms(hid, px, rx, ar_src)

    reduce_steps = reduce.steps()
    for s in range(Y):
        if s < len(reduce_steps):
            reduce_steps[s]()
        each(KVH, lambda g, s=s: scatter.y_step(g, s))
    each(KVH, scatter.z_start)
    for step in reduce_steps[Y:]:
        step()
    each(KVH, lambda g: scatter.finish(g, (pdk, pdv)))
    each(KVH, gather.wait_sends)
    each(KVH, scatter.wait_sends)


def local(
    prefix_input, prefix_query_rows, prefix_key_rows, prefix_value_rows, prefix_output, prefix_output_grad,
    prefix_middle, response_input, response_query, response_key, response_value, response_output,
    response_output_grad, response_middle, lengths, adapter_up_weight,
):
    prefix = Y * ZH * ROWS
    width = 2 * Y * LANES
    vmem = pl.BlockSpec(memory_space=pltpu.VMEM)
    kv_width = KVH * HD
    dma = pltpu.SemaphoreType.DMA
    most = max(Y, ZH * ZL, X) - 1
    small = jax.ShapeDtypeStruct((ROWS, kv_width), BF16)
    outs = pl.pallas_call(
        kernel,
        out_shape=[small, small, small, small, jax.ShapeDtypeStruct((RANK, width), BF16)],
        in_specs=[pl.BlockSpec(memory_space=pltpu.SMEM)] + [vmem] * 15,
        out_specs=[vmem] * 5,
        scratch_shapes=[
            pltpu.VMEM((KVH, 2, prefix, HD), BF16),
            pltpu.VMEM((KVH, 2, prefix, HD), BF16),
            pltpu.VMEM((KVH, Y - 1, 2, ZH * ROWS, HD), BF16),
            pltpu.VMEM((KVH, ZH - 1, 2, ROWS, HD), BF16),
            pltpu.VMEM((QL, HD), BF16),
            pltpu.VMEM((QL, HD), BF16),
            pltpu.VMEM((prefix + ROWS, QL), F32),
            pltpu.VMEM((prefix + ROWS, QL), BF16),
            pltpu.VMEM((prefix + ROWS, QL), BF16),
            pltpu.VMEM((8, HD), F32),
            pltpu.VMEM((RANK, 2 * ROWS), F32),
            pltpu.VMEM((RANK, width), BF16),
            pltpu.VMEM((RANK, width // 2), BF16),
            pltpu.VMEM((X - 1, 16, width // 2), BF16),
            pltpu.VMEM((Y - 1, 16, LANES), BF16),
            pltpu.VMEM((ZH * ZL, 16, LANES), BF16),
            pltpu.VMEM((RANK, width // 2), BF16),
            dma((KVH, ZH - 1)), dma((KVH, ZH - 1)),
            dma((KVH, Y - 1, 2)), dma((KVH, Y - 1, 2)),
            dma((KVH, Y - 1, 2)), dma((KVH, Y - 1, 2)),
            dma((KVH, ZH - 1)), dma((KVH, ZH - 1)),
            dma((7, most)), dma((7, most)),
        ],
        compiler_params=pltpu.CompilerParams(
            collective_id=0, has_side_effects=True, vmem_limit_bytes=56 * 1024 * 1024),
    )(
        lengths, prefix_key_rows[0], prefix_value_rows[0], response_key[0, 0], response_value[0, 0],
        prefix_query_rows[0], response_query[0, 0], prefix_output_grad[0], response_output_grad[0, 0],
        prefix_output[0], response_output[0, 0], prefix_input[0], response_input[0, 0],
        prefix_middle[0], response_middle[0, 0], adapter_up_weight,
    )
    dkey, dvalue, resp_dkey, resp_dvalue, total = outs
    down = 2.0 * total[:, :10 * LANES].astype(F32)
    up = 2.0 * total[:, 10 * LANES:15 * LANES].astype(F32)
    return dkey[None], dvalue[None], resp_dkey[None, None], resp_dvalue[None, None], down.T, up


def solution(mesh):
    rows, slots = P("prompt", "resp", None), P("prompt", "resp", None, None)
    return jax.shard_map(
        local,
        mesh=mesh,
        in_specs=(rows,) * 7 + (slots,) * 7 + (P("prompt", "resp"), P()),
        out_specs=(rows, rows, slots, slots, P(), P()),
        check_vma=False,
    )
```

time: 1130 us -> 178 us (0.16)
  the two profiles are of different devices: /device:TPU:2 before, /device:TPU:16 now
where the time goes in v1:
time: 178 us
  Pallas kernels  170 us (96%)
  other arithmetic  4.15 us (2%)
  local copies, waits for them, and re-layouts  2.53 us (1%)
    pallas_call x1, Pallas kernels, local(): pl.pallas_call(kernel, out_shape=[small, small, small, small, jax.ShapeDt...  170 us

profile of v1, /device:TPU:16, one launch (start us, length us, event | category | flops | bytes accessed | tf_op | source)
XLA Modules:
  0.0 177.8 jit_solution(328506201074124510)
XLA Ops:
  1.3 169.8 %shard_map.199 = (bf16[64,512]{1,0:T(8,128)(2,1)}, bf16[64,512]{1,0:T(8,128)(2,1)}, bf16[64,512]{1,0:T(8,128)(2,1)}, bf16[64,512]{1,0:T(8,128)(2,1)}, bf16[64,8192]{1,0:T(8,128)(2,1)}) custom-call(s32[1,1]{1,0:T(1,128)S(6)} %copy.26.length_ref, bf16[64,512]{1,0:T(8,128)(2,1)} %bitcast.28, bf16[64,512]{1,0:T(8,128)(2,1)} %bitcast.29, ...), custom_call_target="tpu_custom_call" | custom-call | tf_op jit(solution)/shard_map/pallas_call | solution.py:475
  171.1 0.0 copy-start.3
  171.2 0.0 copy-start.2
  171.2 1.9 %convert_multiply_fusion = f32[64,2560]{1,0:T(8,128)} fusion(bf16[64,8192]{1,0:T(8,128)(2,1)} %get-tuple-element.15), kind=kLoop, calls=%fused_computation.1 | loop fusion | flops 327680 | bytes 983040 | tf_op jit(solution)/shard_map/mul | solution.py:514
  173.0 0.0 copy-start.1
  173.1 0.0 copy-start
  173.1 2.3 %multiply_bitcast_fusion = f32[5120,64]{0,1:T(8,128)} fusion(bf16[64,8192]{1,0:T(8,128)(2,1)} %get-tuple-element.15), kind=kLoop, calls=%fused_computation | loop fusion | flops 655360 | bytes 1966080 | tf_op jit(solution)/shard_map/transpose | solution.py:515
  175.3 0.0 copy-done.3
  175.3 0.6 copy.27
  176.0 0.0 copy-done.2
  176.0 0.6 copy.28
  176.6 0.0 copy-done.1
  176.6 0.6 copy.29
  177.2 0.0 copy-done
  177.2 0.6 copy.30
Async XLA Ops:
  171.1 4.2 %copy-start.3 = (bf16[64,512]{1,0:T(8,128)(2,1)S(1)}, bf16[64,512]{1,0:T(8,128)(2,1)}, u32[]{:S(2)}) copy-start(bf16[64,512]{1,0:T(8,128)(2,1)} %get-tuple-element.11) | copy-start | bytes 196612
  171.2 4.8 %copy-start.2 = (bf16[64,512]{1,0:T(8,128)(2,1)S(1)}, bf16[64,512]{1,0:T(8,128)(2,1)}, u32[]{:S(2)}) copy-start(bf16[64,512]{1,0:T(8,128)(2,1)} %get-tuple-element.12) | copy-start | bytes 196612
  173.0 3.5 %copy-start.1 = (bf16[64,512]{1,0:T(8,128)(2,1)S(1)}, bf16[64,512]{1,0:T(8,128)(2,1)}, u32[]{:S(2)}) copy-start(bf16[64,512]{1,0:T(8,128)(2,1)} %get-tuple-element.13) | copy-start | bytes 196612
  173.1 4.2 %copy-start = (bf16[64,512]{1,0:T(8,128)(2,1)S(1)}, bf16[64,512]{1,0:T(8,128)(2,1)}, u32[]{:S(2)}) copy-start(bf16[64,512]{1,0:T(8,128)(2,1)} %get-tuple-element.14) | copy-start | bytes 196612

commit v2 on v0

v2 whole, which is shorter than its diff:
```python
import functools
import math

import jax
import jax.numpy as jnp
from jax import lax
from jax.experimental import pallas as pl
from jax.experimental.pallas import tpu as pltpu
from jax.sharding import PartitionSpec as P

ZL, X, C, Y, ZH = 2, 4, 2, 8, 4
HD = 128
ROWS = 64
KVH = 4
PAIR = 2
GROUPS = 5
RANK = 64
GROUP_LANES = GROUPS * HD
CHUNK = 4 * HD
PIECE = C * Y * CHUNK
PIECES = 1
FAR = 9
DOWN = KVH * GROUP_LANES
DOWN_END = DOWN + 5120
WIDTH = PIECES * PIECE
QL = 2 * ROWS * GROUPS
SCALE = HD ** -0.5
LOG2E = math.log2(math.e)
F32 = jnp.float32
BF16 = jnp.bfloat16
MESH = pl.DeviceIdType.MESH


def mod(a, n):
    return lax.rem(a + n, n)


def nt(a, b):
    return lax.dot_general(a, b, (((1,), (1,)), ((), ())), preferred_element_type=F32)


def nn(a, b):
    return lax.dot_general(a, b, (((1,), (0,)), ((), ())), preferred_element_type=F32)


def tn(a, b):
    return lax.dot_general(a, b, (((0,), (0,)), ((), ())), preferred_element_type=F32)


class Place:
    def __init__(self):
        p, r = lax.axis_index("prompt"), lax.axis_index("resp")
        self.p, self.r = p, r
        self.core = lax.rem(p, C)
        self.x = lax.rem(lax.div(p, C), X)
        self.zl = lax.div(p, C * X)
        self.y = lax.div(r, ZH)
        self.zh = lax.rem(r, ZH)
        self.z = self.zh * ZL + self.zl

    def device(self, core=None, x=None, y=None, z=None):
        core = self.core if core is None else core
        x = self.x if x is None else x
        y = self.y if y is None else y
        z = self.z if z is None else z
        zl, zh = lax.rem(z, ZL), lax.div(z, ZL)
        return {"prompt": (zl * X + x) * C + core, "resp": y * ZH + zh}


def entry_barrier(at):
    barrier = pltpu.get_barrier_semaphore()
    count = 0
    for off in range(1, C):
        pl.semaphore_signal(barrier, inc=1, device_id=at.device(core=mod(at.core + off, C)), device_id_type=MESH)
        count += 1
    for off in range(1, X):
        pl.semaphore_signal(barrier, inc=1, device_id=at.device(x=mod(at.x + off, X)), device_id_type=MESH)
        count += 1
    for off in range(1, Y):
        pl.semaphore_signal(barrier, inc=1, device_id=at.device(y=mod(at.y + off, Y)), device_id_type=MESH)
        count += 1
    for off in range(1, ZH * ZL):
        pl.semaphore_signal(barrier, inc=1, device_id=at.device(z=mod(at.z + off, ZH * ZL)), device_id_type=MESH)
        count += 1
    return lambda: pl.semaphore_wait(barrier, count)


def rcopy(src, dst, send, recv, device):
    return pltpu.make_async_remote_copy(
        src_ref=src, dst_ref=dst, send_sem=send, recv_sem=recv, device_id=device, device_id_type=MESH)


def rows_at(start, count):
    return pl.ds(pl.multiple_of(start, ROWS), count)


def when(condition, body):
    pl.when(condition)(body)


def each(n, body):
    def step(i, carry):
        body(i)
        return carry
    lax.fori_loop(0, n, step, 0)


def hops(which, way):
    return Y // 2 if which == way else Y - 1 - Y // 2


def chains(turn):
    for which in range(2):
        for way in range(2):
            turn(which, way, hops(which, way), 1 if way == 0 else -1)


class Gather:
    def __init__(self, at, kv, zs, zr, ys, yr):
        self.at, self.kv, self.zs, self.zr, self.ys, self.yr = at, kv, zs, zr, ys, yr

    def z_copy(self, h, off, sending):
        at = self.at
        zh = at.zh if sending else mod(at.zh - off, ZH)
        ref = self.kv.at[h, :, at.y, zh]
        target = at.device(z=mod(at.zh + off, ZH) * ZL + at.zl)
        return rcopy(ref, ref, self.zs.at[h, off - 1], self.zr.at[h, off - 1], target)

    def z_start(self, h):
        for off in range(1, ZH):
            self.z_copy(h, off, True).start()

    def z_wait(self, h):
        for off in range(1, ZH):
            self.z_copy(h, off, False).wait_recv()

    def y_copy(self, h, s, which, way, sign, sending):
        at = self.at
        lag = s if sending else s + 1
        ref = self.kv.at[h, which, mod(at.y - sign * lag + Y, Y)]
        return rcopy(ref, ref, self.ys.at[h, s, which, way], self.yr.at[h, s, which, way],
                     at.device(y=mod(at.y + sign, Y)))

    def y_step(self, h, s):
        def turn(which, way, count, sign):
            when((s > 0) & (s <= count), lambda: self.y_copy(h, s - 1, which, way, sign, False).wait_recv())
            when(s < count, lambda: self.y_copy(h, s, which, way, sign, True).start())
        chains(turn)

    def wait_sends(self, h):
        for off in range(1, ZH):
            self.z_copy(h, off, True).wait_send()

        def turn(which, way, count, sign):
            each(count, lambda s: self.y_copy(h, s, which, way, sign, True).wait_send())
        chains(turn)


class Scatter:
    def __init__(self, at, tm, rb, zb, ss, sr, ws, wr, outs):
        self.at, self.tm, self.rb, self.zb = at, tm, rb, zb
        self.ss, self.sr, self.ws, self.wr = ss, sr, ws, wr
        self.outs = outs

    def y_ref(self, h, s, which, count, sign):
        return self.tm.at[h, which, mod(self.at.y + sign * (count - s) + Y, Y)]

    def y_copy(self, h, s, which, way, count, sign):
        return rcopy(self.y_ref(h, s, which, count, sign), self.rb.at[h, s, which, way],
                     self.ss.at[h, s, which, way], self.sr.at[h, s, which, way],
                     self.at.device(y=mod(self.at.y + sign, Y)))

    def y_step(self, h, s):
        def turn(which, way, count, sign):
            def receive():
                self.y_copy(h, s - 1, which, way, count, sign).wait_recv()
                ref = self.y_ref(h, s, which, count, sign)
                ref[...] = (ref[...].astype(F32) + self.rb[h, s - 1, which, way].astype(F32)).astype(BF16)
            when((s > 0) & (s <= count), receive)
            when(s < count, lambda: self.y_copy(h, s, which, way, count, sign).start())
        chains(turn)

    def z_copy(self, h, off):
        at = self.at
        zh = mod(at.zh + off, ZH)
        return rcopy(self.tm.at[h, :, at.y, zh], self.zb.at[h, off - 1], self.ws.at[h, off - 1],
                     self.wr.at[h, off - 1], at.device(z=zh * ZL + at.zl))

    def z_start(self, h):
        for off in range(1, ZH):
            self.z_copy(h, off).start()

    def finish(self, h):
        at = self.at
        for off in range(1, ZH):
            self.z_copy(h, off).wait_recv()
        for which in range(2):
            total = self.tm[h, which, at.y, at.zh].astype(F32)
            for off in range(1, ZH):
                total += self.zb[h, off - 1, which].astype(F32)
            self.outs[which][:, h * HD:(h + 1) * HD] = total.astype(BF16)

    def wait_sends(self, h):
        for off in range(1, ZH):
            self.z_copy(h, off).wait_send()

        def turn(which, way, count, sign):
            each(count, lambda s: self.y_copy(h, s, which, way, count, sign).wait_send())
        chains(turn)


class Reduce:
    def __init__(self, at, src, out, rc, rx, ry, rz, part, send, recv):
        self.at, self.src, self.out = at, src, out
        self.rc, self.rx, self.ry, self.rz, self.part = rc, rx, ry, rz, part
        self.send, self.recv = send, recv
        self.n = ZH * ZL

    def rows(self, x):
        return pl.ds(pl.multiple_of(x * 16, 16), 16)

    def half(self, i, core):
        return pl.ds(pl.multiple_of(i * PIECE + core * (PIECE // 2), HD), PIECE // 2)

    def lanes(self, i, core, y):
        return pl.ds(pl.multiple_of(i * PIECE + core * (PIECE // 2) + y * CHUNK, HD), CHUNK)

    def chunk(self, y):
        return pl.ds(pl.multiple_of(y * CHUNK, HD), CHUNK)

    def sems(self, i, step, off):
        return self.send.at[i, step, off - 1], self.recv.at[i, step, off - 1]

    def core_copy(self, i):
        other = mod(self.at.core + 1, C)
        return rcopy(self.src.at[:, self.half(i, other)], self.rc.at[i], *self.sems(i, 0, 1),
                     self.at.device(core=other))

    def x_copy(self, i, off):
        x = mod(self.at.x + off, X)
        return rcopy(self.part.at[i, self.rows(x), :], self.rx.at[i, off - 1], *self.sems(i, 1, off),
                     self.at.device(x=x))

    def y_copy(self, i, off):
        y = mod(self.at.y + off, Y)
        return rcopy(self.part.at[i, self.rows(self.at.x), self.chunk(y)], self.ry.at[i, off - 1],
                     *self.sems(i, 2, off), self.at.device(y=y))

    def z_copy(self, i, off, sending):
        z = self.at.z if sending else mod(self.at.z - off, self.n)
        return rcopy(self.rz.at[i, z], self.rz.at[i, z], *self.sems(i, 3, off),
                     self.at.device(z=mod(self.at.z + off, self.n)))

    def y_back(self, i, off, sending):
        y = self.at.y if sending else mod(self.at.y - off, Y)
        ref = self.out.at[self.rows(self.at.x), self.lanes(i, self.at.core, y)]
        return rcopy(ref, ref, *self.sems(i, 4, off), self.at.device(y=mod(self.at.y + off, Y)))

    def x_back(self, i, off, sending):
        x = self.at.x if sending else mod(self.at.x - off, X)
        ref = self.out.at[self.rows(x), self.half(i, self.at.core)]
        return rcopy(ref, ref, *self.sems(i, 5, off), self.at.device(x=mod(self.at.x + off, X)))

    def core_back(self, i, sending):
        core = self.at.core if sending else mod(self.at.core + 1, C)
        ref = self.out.at[:, self.half(i, core)]
        return rcopy(ref, ref, *self.sems(i, 6, 1), self.at.device(core=mod(self.at.core + 1, C)))

    def step(self, i, k):
        at = self.at
        if k == 0:
            self.core_copy(i).start()
        if k == 1:
            self.core_copy(i).wait_recv()
            self.part[i] = (self.src[:, self.half(i, at.core)].astype(F32) + self.rc[i].astype(F32)).astype(BF16)
            for off in range(1, X):
                self.x_copy(i, off).start()
        if k == 2:
            total = self.part[i, self.rows(at.x), :].astype(F32)
            for off in range(1, X):
                self.x_copy(i, off).wait_recv()
                total += self.rx[i, off - 1].astype(F32)
            self.part[i, self.rows(at.x), :] = total.astype(BF16)
            for off in range(1, Y):
                self.y_copy(i, off).start()
        if k == 3:
            total = self.part[i, self.rows(at.x), self.chunk(at.y)].astype(F32)
            for off in range(1, Y):
                self.y_copy(i, off).wait_recv()
                total += self.ry[i, off - 1].astype(F32)
            self.rz[i, at.z] = total.astype(BF16)
            for off in range(1, self.n):
                self.z_copy(i, off, True).start()
        if k == 4:
            for off in range(1, self.n):
                self.z_copy(i, off, False).wait_recv()
            total = self.rz[i, 0].astype(F32)
            for z in range(1, self.n):
                total += self.rz[i, z].astype(F32)
            self.out[self.rows(at.x), self.lanes(i, at.core, at.y)] = total.astype(BF16)
            for off in range(1, Y):
                self.y_back(i, off, True).start()
        if k == 5:
            for off in range(1, Y):
                self.y_back(i, off, False).wait_recv()
            for off in range(1, X):
                self.x_back(i, off, True).start()
        if k == 6:
            for off in range(1, X):
                self.x_back(i, off, False).wait_recv()
            self.core_back(i, True).start()
        if k == 7:
            self.core_back(i, False).wait_recv()

    def wait_sends(self, i):
        self.core_copy(i).wait_send()
        self.core_back(i, True).wait_send()
        for off in range(1, X):
            self.x_copy(i, off).wait_send()
            self.x_back(i, off, True).wait_send()
        for off in range(1, Y):
            self.y_copy(i, off).wait_send()
            self.y_back(i, off, True).wait_send()
        for off in range(1, self.n):
            self.z_copy(i, off, True).wait_send()


class Attention:
    def __init__(self, at, length, refs, kv, tm, scr):
        self.at, self.length, self.kv, self.tm = at, length, kv, tm
        (self.pq, self.rq, self.pdo, self.rdo, self.po, self.ro, self.rk, self.rv, self.up_w, self.mid_t) = refs
        (self.qs, self.dos, self.delta, self.s, self.e, self.t, self.hid, self.ar_src, self.rdk, self.rdv) = scr
        self.chunk = PAIR * ZH * ROWS
        self.prefix = Y * ZH * ROWS
        lane = lax.broadcasted_iota(jnp.int32, (1, QL), 1)
        self.in_head = lax.rem(lane, 2 * ROWS)

    def keys(self, h, which, c):
        return self.kv[h, which, pl.ds(c * PAIR, PAIR)].reshape(self.chunk, HD)

    def lanes(self, h):
        return pl.ds(pl.multiple_of(h * HD, HD), HD)

    def q_lanes(self, h, i):
        return pl.ds(pl.multiple_of(h * GROUP_LANES + i * HD, HD), HD)

    def rows_of(self, c):
        return pl.ds(pl.multiple_of(c * self.chunk, self.chunk), self.chunk)

    def prepare(self, h):
        alive = lax.broadcasted_iota(jnp.int32, (ROWS, HD), 0) < self.length
        for i in range(GROUPS):
            lanes = self.q_lanes(h, i)
            top, low = pl.ds(2 * i * ROWS, ROWS), pl.ds((2 * i + 1) * ROWS, ROWS)
            self.qs[h, top, :] = self.pq[:, lanes]
            self.qs[h, low, :] = self.rq[:, lanes]
            grad_top = self.pdo[:, lanes].astype(F32)
            grad_low = jnp.where(alive, self.rdo[:, lanes].astype(F32), 0.0)
            self.dos[h, top, :] = grad_top.astype(BF16)
            self.dos[h, low, :] = grad_low.astype(BF16)
            both = jnp.concatenate(
                [grad_top * self.po[:, lanes].astype(F32), grad_low * self.ro[:, lanes].astype(F32)], axis=0)
            self.delta[h, :, i * HD:(i + 1) * HD] = jnp.sum(both.T, axis=0, keepdims=True)

    def top8(self, s, op):
        return op(s.reshape(s.shape[0] // 8, 8, QL), axis=0)

    def scores(self, h, tick):
        q = self.qs[h]
        limit = jnp.where(self.in_head < ROWS, self.at.r * ROWS + self.in_head, self.prefix)
        own_row = lax.broadcasted_iota(jnp.int32, (ROWS, QL), 0)
        row = lax.broadcasted_iota(jnp.int32, (self.chunk, QL), 0)
        s = jnp.where(own_row <= self.in_head - ROWS, nt(self.rk[:, self.lanes(h)], q), -jnp.inf)
        self.s[pl.ds(self.prefix, ROWS), :] = s

        def body(c, m8):
            tick(c)
            s = jnp.where(row + c * self.chunk <= limit, nt(self.keys(h, 0, c), q), -jnp.inf)
            self.s[self.rows_of(c), :] = s
            return jnp.maximum(m8, self.top8(s, jnp.max))

        m8 = lax.fori_loop(0, Y // PAIR, body, self.top8(s, jnp.max))
        return jnp.max(m8, axis=0, keepdims=True) * (SCALE * LOG2E)

    def weights(self, h, slot, m, tick):
        do, delta = self.dos[h], self.delta[h]

        def part(at_c, k, v):
            e = jnp.exp2(self.s[at_c, :] * (SCALE * LOG2E) - m)
            t = (e * (nt(v, do) - delta)).astype(BF16)
            self.e[slot, at_c, :] = e.astype(BF16)
            self.t[slot, at_c, :] = t
            return self.top8(e, jnp.sum), tn(k, t)

        def body(c, carry):
            tick(c)
            l8, dq = part(self.rows_of(c), self.keys(h, 0, c), self.keys(h, 1, c))
            return carry[0] + l8, carry[1] + dq

        own = part(pl.ds(self.prefix, ROWS), self.rk[:, self.lanes(h)], self.rv[:, self.lanes(h)])
        l8, dq = lax.fori_loop(0, Y // PAIR, body, own)
        inv = 1.0 / jnp.sum(l8, axis=0, keepdims=True)
        inv_col = jnp.concatenate(
            [jnp.broadcast_to(inv[:, i * HD:(i + 1) * HD], (HD, HD)).T for i in range(GROUPS)], axis=0)
        self.qs[h] = (self.qs[h].astype(F32) * (inv_col * SCALE)).astype(BF16)
        self.dos[h] = (self.dos[h].astype(F32) * inv_col).astype(BF16)
        dq_low = (dq * (inv * SCALE)).astype(BF16)
        hidden = self.hid[...]
        for i in range(GROUPS):
            piece = dq_low[:, i * HD:(i + 1) * HD]
            hidden += nn(self.up_w[:, self.q_lanes(h, i)], piece)
            lanes = self.q_lanes(h, i)
            self.ar_src[:, lanes] = nt(self.mid_t[...], piece).astype(BF16)
        self.hid[...] = hidden

    def terms(self, h, slot, tick):
        q, do = self.qs[h], self.dos[h]

        def body(c, carry):
            tick(c)
            at_c = self.rows_of(c)
            shape = (PAIR, ZH, ROWS, HD)
            self.tm[h, 0, pl.ds(c * PAIR, PAIR)] = nn(self.t[slot, at_c, :], q).astype(BF16).reshape(shape)
            self.tm[h, 1, pl.ds(c * PAIR, PAIR)] = nn(self.e[slot, at_c, :], do).astype(BF16).reshape(shape)
            return carry

        lax.fori_loop(0, Y // PAIR, body, 0)
        own = pl.ds(self.prefix, ROWS)
        self.rdk[:, self.lanes(h)] = nn(self.t[slot, own, :], q).astype(BF16)
        self.rdv[:, self.lanes(h)] = nn(self.e[slot, own, :], do).astype(BF16)


def down_terms(hid, px, rx, ar_src):
    hidden = hid[...].astype(BF16)
    for j in range(0, DOWN_END - DOWN, 512):
        lanes = slice(j, j + 512)
        ar_src[:, DOWN + j:DOWN + j + 512] = (
            nn(hidden[:, :ROWS], px[:, lanes]) + nn(hidden[:, ROWS:], rx[:, lanes])).astype(BF16)


def kernel(length_ref, pk, pv, rk, rv, pm, rm, *rest):
    far, rest = rest[:FAR], rest[FAR:]
    (pdk, pdv, rdk, rdv, total), rest = rest[:5], rest[5:]
    near, rest = rest[:FAR], rest[FAR:]
    (kv, tm, rb, zb, qs, dos, delta, s_scr, e_scr, t_scr, hid, mid_t, ar_src, rc, rx_b, ry, rz, part,
     gzs, gzr, gys, gyr, sys, syr, szs, szr, asend, arecv, loaded) = rest
    pq, rq, pdo, rdo, po, ro, up_w, px, rx = near
    at = Place()
    gather = Gather(at, kv, gzs, gzr, gys, gyr)
    scatter = Scatter(at, tm, rb, zb, sys, syr, szs, szr, (pdk, pdv))
    reduce = Reduce(at, ar_src, total, rc, rx_b, ry, rz, part, asend, arecv)
    refs = (pq, rq, pdo, rdo, po, ro, rk, rv, up_w, mid_t)
    scr = (qs, dos, delta, s_scr, e_scr, t_scr, hid, ar_src, rdk, rdv)
    attention = Attention(at, length_ref[0, 0], refs, kv, tm, scr)
    parts = Y // PAIR
    last = Y // 2

    everyone_in = entry_barrier(at)
    loads = [pltpu.make_async_copy(far[i], near[i], loaded.at[i]) for i in range(FAR)]
    for load in loads:
        load.start()
    for h in range(KVH):
        kv[h, 0, at.y, at.zh] = pk[:, h * HD:(h + 1) * HD]
        kv[h, 1, at.y, at.zh] = pv[:, h * HD:(h + 1) * HD]
    everyone_in()
    each(KVH, gather.z_start)
    hid[...] = jnp.zeros_like(hid)
    ar_src[:, DOWN_END:] = jnp.zeros((RANK, WIDTH - DOWN_END), BF16)
    mid_t[...] = jnp.concatenate([pm[...].astype(F32).T, rm[...].astype(F32).T], axis=1).astype(BF16)

    for load in loads:
        load.wait()

    def begin(h):
        gather.z_wait(h)
        gather.y_step(h, 0)
    each(2, begin)

    def first(s):
        attention.prepare(s)
        each(2, lambda h: gather.y_step(h, s + 1))
    each(last, first)
    each(2, lambda i: begin(i + 2))

    def second(h):
        def tick(unit):
            def at_part(c):
                slot = (h * 3 + unit) * parts + c

                def events():
                    s = lax.div(slot, 5)
                    each(2, lambda i: gather.y_step(i + 2, s))
                when((lax.rem(slot, 5) == 0) & (slot > 0), events)
                when(slot == 17, lambda: scatter.y_step(0, 0))
            return at_part
        m = attention.scores(h, tick(0))
        attention.weights(h, h, m, tick(1))
        attention.terms(h, h, tick(2))
    each(2, second)

    def third(i):
        def tick(unit):
            def at_part(c):
                slot = (i * 2 + unit) * parts + c

                def events():
                    s = lax.div(slot, 8)
                    scatter.y_step(0, s + 1)
                    scatter.y_step(1, s)
                when(lax.rem(slot, 8) == 0, events)
            return at_part
        m = attention.scores(i + 2, tick(0))
        attention.weights(i + 2, i, m, tick(1))
    each(2, third)

    def sums(k):
        each(PIECES, lambda i: reduce.step(i, k))

    down_terms(hid, px, rx, ar_src)
    sums(0)
    attention.terms(2, 0, lambda c: None)
    scatter.y_step(0, 3)
    scatter.y_step(1, 2)
    scatter.y_step(2, 0)
    sums(1)
    attention.terms(3, 1, lambda c: None)
    scatter.y_step(3, 0)
    scatter.y_step(0, 4)
    scatter.z_start(0)
    sums(2)
    scatter.y_step(1, 3)
    scatter.y_step(2, 1)
    sums(3)
    scatter.y_step(3, 1)
    scatter.y_step(1, 4)
    scatter.z_start(1)
    sums(4)
    scatter.y_step(2, 2)
    scatter.y_step(3, 2)
    sums(5)
    scatter.y_step(2, 3)
    scatter.y_step(3, 3)
    sums(6)
    scatter.y_step(2, 4)
    scatter.z_start(2)
    scatter.y_step(3, 4)
    scatter.z_start(3)
    sums(7)
    for h in range(KVH):
        scatter.finish(h)
    each(KVH, gather.wait_sends)
    each(KVH, scatter.wait_sends)
    each(PIECES, reduce.wait_sends)


def results(total, pdk, pdv, rdk, rdv, down, up, *low):
    for src, dst in zip((pdk, pdv, rdk, rdv), low):
        dst[...] = src[...]
    down[...] = 2.0 * total[:, DOWN:DOWN_END].astype(F32)
    up[...] = 2.0 * total[:, :DOWN].astype(F32)


def local(
    prefix_input, prefix_query_rows, prefix_key_rows, prefix_value_rows, prefix_output, prefix_output_grad,
    prefix_middle, response_input, response_query, response_key, response_value, response_output,
    response_output_grad, response_middle, lengths, adapter_up_weight,
):
    prefix = Y * ZH * ROWS
    width = WIDTH
    vmem = pl.BlockSpec(memory_space=pltpu.VMEM)
    kv_width = KVH * HD
    dma = pltpu.SemaphoreType.DMA
    most = max(Y, ZH * ZL, X) - 1
    small = jax.ShapeDtypeStruct((ROWS, kv_width), BF16)
    far = (prefix_query_rows[0], response_query[0, 0], prefix_output_grad[0], response_output_grad[0, 0],
           prefix_output[0], response_output[0, 0], adapter_up_weight, prefix_input[0], response_input[0, 0])
    outs = pl.pallas_call(
        kernel,
        out_shape=[small, small, small, small, jax.ShapeDtypeStruct((RANK, width), BF16)],
        in_specs=[pl.BlockSpec(memory_space=pltpu.SMEM)] + [vmem] * 6 + [pl.BlockSpec(memory_space=pl.ANY)] * FAR,
        out_specs=[vmem] * 5,
        scratch_shapes=[pltpu.VMEM(a.shape, BF16) for a in far] + [
            pltpu.VMEM((KVH, 2, Y, ZH, ROWS, HD), BF16),
            pltpu.VMEM((KVH, 2, Y, ZH, ROWS, HD), BF16),
            pltpu.VMEM((KVH, Y // 2, 2, 2, ZH, ROWS, HD), BF16),
            pltpu.VMEM((KVH, ZH - 1, 2, ROWS, HD), BF16),
            pltpu.VMEM((KVH, QL, HD), BF16),
            pltpu.VMEM((KVH, QL, HD), BF16),
            pltpu.VMEM((KVH, 1, QL), F32),
            pltpu.VMEM((prefix + ROWS, QL), F32),
            pltpu.VMEM((2, prefix + ROWS, QL), BF16),
            pltpu.VMEM((2, prefix + ROWS, QL), BF16),
            pltpu.VMEM((RANK, 2 * ROWS), F32),
            pltpu.VMEM((RANK, 2 * ROWS), BF16),
            pltpu.VMEM((RANK, width), BF16),
            pltpu.VMEM((PIECES, RANK, PIECE // 2), BF16),
            pltpu.VMEM((PIECES, X - 1, 16, PIECE // 2), BF16),
            pltpu.VMEM((PIECES, Y - 1, 16, CHUNK), BF16),
            pltpu.VMEM((PIECES, ZH * ZL, 16, CHUNK), BF16),
            pltpu.VMEM((PIECES, RANK, PIECE // 2), BF16),
            dma((KVH, ZH - 1)), dma((KVH, ZH - 1)),
            dma((KVH, Y // 2, 2, 2)), dma((KVH, Y // 2, 2, 2)),
            dma((KVH, Y // 2, 2, 2)), dma((KVH, Y // 2, 2, 2)),
            dma((KVH, ZH - 1)), dma((KVH, ZH - 1)),
            dma((PIECES, 7, most)), dma((PIECES, 7, most)), dma((FAR,)),
        ],
        compiler_params=pltpu.CompilerParams(
            collective_id=0, has_side_effects=True, vmem_limit_bytes=56 * 1024 * 1024),
    )(
        lengths, prefix_key_rows[0], prefix_value_rows[0], response_key[0, 0], response_value[0, 0],
        prefix_middle[0], response_middle[0, 0], *far,
    )
    dkey, dvalue, resp_dkey, resp_dvalue, total = outs
    down, up, dkey, dvalue, resp_dkey, resp_dvalue = pl.pallas_call(
        results,
        out_shape=[jax.ShapeDtypeStruct((RANK, DOWN_END - DOWN), F32),
                   jax.ShapeDtypeStruct((RANK, KVH * GROUP_LANES), F32), small, small, small, small],
        in_specs=[vmem] * 5,
        out_specs=[vmem] * 6,
    )(total, dkey, dvalue, resp_dkey, resp_dvalue)
    return dkey[None], dvalue[None], resp_dkey[None, None], resp_dvalue[None, None], down.T, up


def solution(mesh):
    rows, slots = P("prompt", "resp", None), P("prompt", "resp", None, None)
    return jax.shard_map(
        local,
        mesh=mesh,
        in_specs=(rows,) * 7 + (slots,) * 7 + (P("prompt", "resp"), P()),
        out_specs=(rows, rows, slots, slots, P(), P()),
        check_vma=False,
    )
```

time: 1130 us -> 139 us (0.12)
  the two profiles are of different devices: /device:TPU:2 before, /device:TPU:4 now
where the time goes in v2:
time: 139 us; the launch traced here: 138 us
  Pallas kernels  137 us (99%)
    pallas_call x1, Pallas kernels, local(): pl.pallas_call(kernel, out_shape=[small, small, small, small, jax.ShapeDt...  135 us

profile of v2, /device:TPU:4, one launch (start us, length us, event | category | flops | bytes accessed | tf_op | source)
XLA Modules:
  0.0 138.5 jit_solution(185322178644009083)
XLA Ops:
  1.3 134.5 %shard_map.199 = (bf16[64,512]{1,0:T(8,128)(2,1)}, bf16[64,512]{1,0:T(8,128)(2,1)}, bf16[64,512]{1,0:T(8,128)(2,1)}, bf16[64,512]{1,0:T(8,128)(2,1)}, bf16[64,8192]{1,0:T(8,128)(2,1)}) custom-call(s32[1,1]{1,0:T(1,128)S(6)} %copy.22.length_ref, bf16[64,512]{1,0:T(8,128)(2,1)} %bitcast.27, bf16[64,512]{1,0:T(8,128)(2,1)} %bitcast.28, ...), custom_call_target="tpu_custom_call" | custom-call | tf_op jit(solution)/shard_map/pallas_call | solution.py:577
  135.8 2.7 %shard_map.200 = (f32[64,5120]{1,0:T(8,128)}, f32[64,2560]{1,0:T(8,128)}, bf16[64,512]{1,0:T(8,128)(2,1)}, bf16[64,512]{1,0:T(8,128)(2,1)}, bf16[64,512]{1,0:T(8,128)(2,1)}, /*index=5*/bf16[64,512]{1,0:T(8,128)(2,1)}) custom-call(bf16[64,8192]{1,0:T(8,128)(2,1)} %get-tuple-element.17.total, bf16[64,512]{1,0:T(8,128)(2,1)} %get-tuple-element.18.pdk, ...), custom_call_target="tpu_custom_call" | custom-call | tf_op jit(solution)/shard_map/pallas_call | solution.py:614

commit v3 on v2

--- a/solution.py
+++ b/solution.py
@@ -210,9 +210,9 @@
 
 
 class Reduce:
-    def __init__(self, at, src, out, rc, rx, ry, rz, part, send, recv):
+    def __init__(self, at, src, out, rc, rx, rz, ry, part, send, recv):
         self.at, self.src, self.out = at, src, out
-        self.rc, self.rx, self.ry, self.rz, self.part = rc, rx, ry, rz, part
+        self.rc, self.rx, self.rz, self.ry, self.part = rc, rx, rz, ry, part
         self.send, self.recv = send, recv
         self.n = ZH * ZL
 
@@ -222,11 +222,11 @@
     def half(self, i, core):
         return pl.ds(pl.multiple_of(i * PIECE + core * (PIECE // 2), HD), PIECE // 2)
 
-    def lanes(self, i, core, y):
-        return pl.ds(pl.multiple_of(i * PIECE + core * (PIECE // 2) + y * CHUNK, HD), CHUNK)
-
-    def chunk(self, y):
-        return pl.ds(pl.multiple_of(y * CHUNK, HD), CHUNK)
+    def lanes(self, i, core, z):
+        return pl.ds(pl.multiple_of(i * PIECE + core * (PIECE // 2) + z * CHUNK, HD), CHUNK)
+
+    def chunk(self, z):
+        return pl.ds(pl.multiple_of(z * CHUNK, HD), CHUNK)
 
     def sems(self, i, step, off):
         return self.send.at[i, step, off - 1], self.recv.at[i, step, off - 1]
@@ -241,20 +241,20 @@
         return rcopy(self.part.at[i, self.rows(x), :], self.rx.at[i, off - 1], *self.sems(i, 1, off),
                      self.at.device(x=x))
 
-    def y_copy(self, i, off):
-        y = mod(self.at.y + off, Y)
-        return rcopy(self.part.at[i, self.rows(self.at.x), self.chunk(y)], self.ry.at[i, off - 1],
-                     *self.sems(i, 2, off), self.at.device(y=y))
-
-    def z_copy(self, i, off, sending):
+    def z_copy(self, i, off):
+        z = mod(self.at.z + off, self.n)
+        return rcopy(self.part.at[i, self.rows(self.at.x), self.chunk(z)], self.rz.at[i, off - 1],
+                     *self.sems(i, 2, off), self.at.device(z=z))
+
+    def y_copy(self, i, off, sending):
+        y = self.at.y if sending else mod(self.at.y - off, Y)
+        return rcopy(self.ry.at[i, y], self.ry.at[i, y], *self.sems(i, 3, off),
+                     self.at.device(y=mod(self.at.y + off, Y)))
+
+    def z_back(self, i, off, sending):
         z = self.at.z if sending else mod(self.at.z - off, self.n)
-        return rcopy(self.rz.at[i, z], self.rz.at[i, z], *self.sems(i, 3, off),
-                     self.at.device(z=mod(self.at.z + off, self.n)))
-
-    def y_back(self, i, off, sending):
-        y = self.at.y if sending else mod(self.at.y - off, Y)
-        ref = self.out.at[self.rows(self.at.x), self.lanes(i, self.at.core, y)]
-        return rcopy(ref, ref, *self.sems(i, 4, off), self.at.device(y=mod(self.at.y + off, Y)))
+        ref = self.out.at[self.rows(self.at.x), self.lanes(i, self.at.core, z)]
+        return rcopy(ref, ref, *self.sems(i, 4, off), self.at.device(z=mod(self.at.z + off, self.n)))
 
     def x_back(self, i, off, sending):
         x = self.at.x if sending else mod(self.at.x - off, X)
@@ -281,28 +281,28 @@
                 self.x_copy(i, off).wait_recv()
                 total += self.rx[i, off - 1].astype(F32)
             self.part[i, self.rows(at.x), :] = total.astype(BF16)
+            for off in range(1, self.n):
+                self.z_copy(i, off).start()
+        if k == 3:
+            total = self.part[i, self.rows(at.x), self.chunk(at.z)].astype(F32)
+            for off in range(1, self.n):
+                self.z_copy(i, off).wait_recv()
+                total += self.rz[i, off - 1].astype(F32)
+            self.ry[i, at.y] = total.astype(BF16)
             for off in range(1, Y):
-                self.y_copy(i, off).start()
-        if k == 3:
-            total = self.part[i, self.rows(at.x), self.chunk(at.y)].astype(F32)
+                self.y_copy(i, off, True).start()
+        if k == 4:
             for off in range(1, Y):
-                self.y_copy(i, off).wait_recv()
-                total += self.ry[i, off - 1].astype(F32)
-            self.rz[i, at.z] = total.astype(BF16)
+                self.y_copy(i, off, False).wait_recv()
+            total = self.ry[i, 0].astype(F32)
+            for y in range(1, Y):
+                total += self.ry[i, y].astype(F32)
+            self.out[self.rows(at.x), self.lanes(i, at.core, at.z)] = total.astype(BF16)
             for off in range(1, self.n):
-                self.z_copy(i, off, True).start()
-        if k == 4:
+                self.z_back(i, off, True).start()
+        if k == 5:
             for off in range(1, self.n):
-                self.z_copy(i, off, False).wait_recv()
-            total = self.rz[i, 0].astype(F32)
-            for z in range(1, self.n):
-                total += self.rz[i, z].astype(F32)
-            self.out[self.rows(at.x), self.lanes(i, at.core, at.y)] = total.astype(BF16)
-            for off in range(1, Y):
-                self.y_back(i, off, True).start()
-        if k == 5:
-            for off in range(1, Y):
-                self.y_back(i, off, False).wait_recv()
+                self.z_back(i, off, False).wait_recv()
             for off in range(1, X):
                 self.x_back(i, off, True).start()
         if k == 6:
@@ -318,11 +318,11 @@
         for off in range(1, X):
             self.x_copy(i, off).wait_send()
             self.x_back(i, off, True).wait_send()
+        for off in range(1, self.n):
+            self.z_copy(i, off).wait_send()
+            self.z_back(i, off, True).wait_send()
         for off in range(1, Y):
-            self.y_copy(i, off).wait_send()
-            self.y_back(i, off, True).wait_send()
-        for off in range(1, self.n):
-            self.z_copy(i, off, True).wait_send()
+            self.y_copy(i, off, True).wait_send()
 
 
 class Attention:
@@ -479,39 +479,37 @@
     def first(s):
         attention.prepare(s)
         each(2, lambda h: gather.y_step(h, s + 1))
-    each(last, first)
+    each(last - 1, first)
     each(2, lambda i: begin(i + 2))
+    first(last - 1)
 
     def second(h):
         def tick(unit):
             def at_part(c):
                 slot = (h * 3 + unit) * parts + c
 
-                def events():
-                    s = lax.div(slot, 5)
-                    each(2, lambda i: gather.y_step(i + 2, s))
-                when((lax.rem(slot, 5) == 0) & (slot > 0), events)
-                when(slot == 17, lambda: scatter.y_step(0, 0))
+                when((slot < 18) & (lax.rem(slot, 7) == 2), lambda: gather.y_step(2, lax.div(slot, 7) + 1))
+                when(slot == 5, lambda: gather.y_step(3, 1))
+                when(slot == 14, lambda: gather.y_step(3, 2))
             return at_part
         m = attention.scores(h, tick(0))
         attention.weights(h, h, m, tick(1))
         attention.terms(h, h, tick(2))
     each(2, second)
 
-    def third(i):
-        def tick(unit):
-            def at_part(c):
-                slot = (i * 2 + unit) * parts + c
-
-                def events():
-                    s = lax.div(slot, 8)
-                    scatter.y_step(0, s + 1)
-                    scatter.y_step(1, s)
-                when(lax.rem(slot, 8) == 0, events)
-            return at_part
-        m = attention.scores(i + 2, tick(0))
-        attention.weights(i + 2, i, m, tick(1))
-    each(2, third)
+    gather.y_step(2, last)
+    gather.y_step(3, last - 1)
+    scatter.y_step(0, 0)
+    m = attention.scores(2, lambda c: None)
+    scatter.y_step(1, 0)
+    attention.weights(2, 0, m, lambda c: None)
+    gather.y_step(3, last)
+
+    scatter.y_step(0, 1)
+    m = attention.scores(3, lambda c: None)
+    scatter.y_step(1, 1)
+    scatter.y_step(0, 2)
+    attention.weights(3, 1, m, lambda c: None)
 
     def sums(k):
         each(PIECES, lambda i: reduce.step(i, k))

time: 139 us -> 134 us (0.964)
  the two profiles are of different devices: /device:TPU:4 before, /device:TPU:16 now
where the time goes in v3:
time: 134 us; the launch traced here: 133 us
  Pallas kernels  132 us (99%)
    pallas_call x1, Pallas kernels, local(): pl.pallas_call(kernel, out_shape=[small, small, small, small, jax.ShapeDt...  130 us
    pallas_call x1, Pallas kernels, local(): pl.pallas_call(results, out_shape=[jax.ShapeDtypeStruct((RANK, DOWN_END -...  2.69 us

profile of v3, /device:TPU:16, one launch (start us, length us, event | category | flops | bytes accessed | tf_op | source)
XLA Modules:
  0.0 133.5 jit_solution(9914732826483055513)
XLA Ops:
  1.3 129.5 %shard_map.199 = (bf16[64,512]{1,0:T(8,128)(2,1)}, bf16[64,512]{1,0:T(8,128)(2,1)}, bf16[64,512]{1,0:T(8,128)(2,1)}, bf16[64,512]{1,0:T(8,128)(2,1)}, bf16[64,8192]{1,0:T(8,128)(2,1)}) custom-call(s32[1,1]{1,0:T(1,128)S(6)} %copy.22.length_ref, bf16[64,512]{1,0:T(8,128)(2,1)} %bitcast.27, bf16[64,512]{1,0:T(8,128)(2,1)} %bitcast.28, ...), custom_call_target="tpu_custom_call" | custom-call | tf_op jit(solution)/shard_map/pallas_call | solution.py:575
  130.8 2.7 %shard_map.200 = (f32[64,5120]{1,0:T(8,128)}, f32[64,2560]{1,0:T(8,128)}, bf16[64,512]{1,0:T(8,128)(2,1)}, bf16[64,512]{1,0:T(8,128)(2,1)}, bf16[64,512]{1,0:T(8,128)(2,1)}, /*index=5*/bf16[64,512]{1,0:T(8,128)(2,1)}) custom-call(bf16[64,8192]{1,0:T(8,128)(2,1)} %get-tuple-element.17.total, bf16[64,512]{1,0:T(8,128)(2,1)} %get-tuple-element.18.pdk, ...), custom_call_target="tpu_custom_call" | custom-call | tf_op jit(solution)/shard_map/pallas_call | solution.py:612
